TPU v7x, 32 devices: a whole 2x2x4 slice. The times are simulated.
32 devices in a mesh: ctx: 4 (over z), enc: 4 (over y, core), mp: 2 (over x).
Axes of the slice: x: 2, y: 2, z: 4, core: 2. Of those that a mesh axis runs over, the one named last changes fastest.
Arguments:
- hidden_in: bfloat16 [1024, 4096], P('ctx'), may hold values from -6 to 6
- norm_gains: float32 [2, 4096], replicated, may hold values from 0.5 to 1.5
- w_cross_query: bfloat16 [4096, 2048], P('ctx', ('enc', 'mp')), may hold values from -1 to 1
- w_cross_out: bfloat16 [2048, 4096], P(('enc', 'mp'), 'ctx'), may hold values from -0.125 to 0.125
- w_self_qkv: bfloat16 [4096, 3, 2048], P('ctx', None, ('enc', 'mp')), may hold values from -1 to 1
- w_self_out: bfloat16 [2048, 4096], P(('enc', 'mp'), 'ctx'), may hold values from -0.125 to 0.125
- nbr_kv: bfloat16 [4, 4, 4, 3, 64, 1024], P('ctx', 'enc', None, None, None, 'mp'), may hold values from -6 to 6
- nbr_count: int32 [16], P('ctx'), may hold values from 1 to 2
- nbr_source: int32 [16, 2], P('ctx'), may hold values from 0 to 3, all different within a row; in each aligned block of 4 rows (0 to 3, 4 to 7, ...) at most 3 rows name the same one
- span_order: int32 [16], replicated, may hold values from 0 to 15, each once
Outputs:
- block_out: bfloat16 [1024, 4096], P('ctx', ('enc', 'mp'))
Inputs may be any that keep to these rules, and one draw needn't show every extreme that they name: `nbr_source`: within the 4 stored spans of one index of ctx (aligned blocks of rows), no encoder index is named more than 3 times, and one is named exactly 3 times in some block; the 2 entries of a span differ. `span_order`: each of the 16 positions appears once.
All inputs are finite; a program needn't handle non-finite values.
Results may differ from a plain program's by a relative error of at most 0.015.
Values may be sent and summed in bfloat16 or wider, within the bound.
A program may use at most 128 MiB of HBM per device.

v0:
```python
import functools
import math

import jax
import jax.numpy as jnp
from jax import lax
from jax.experimental import pallas as pl
from jax.experimental.pallas import tpu as pltpu
from jax.sharding import PartitionSpec as P

MESH = pl.DeviceIdType.MESH
VMEM_GRANT = 56 * 1024 * 1024
BF16 = jnp.bfloat16
F32 = jnp.float32

HD = 128
SPAN = 64


epsilon = 1e-05
far_below = -1e30


def rms_rows(row_values, gain_row):
    values = row_values.astype(jnp.float32)
    row_scale = lax.rsqrt(jnp.mean(values * values, axis=-1, keepdims=True) + epsilon)
    return (values * row_scale * gain_row).astype(jnp.bfloat16)


def token_places(order_table, first_row, row_count):
    tokens = first_row + jnp.arange(row_count, dtype=jnp.int32)
    blocks = tokens // SPAN
    matches = blocks[:, None] == jnp.arange(order_table.shape[0], dtype=jnp.int32)[None, :]
    placed = jnp.sum(jnp.where(matches, order_table[None, :], 0), axis=1)
    return placed * SPAN + tokens % SPAN


def per_device(
    hidden_in,
    norm_gains,
    w_cross_query,
    w_cross_out,
    w_self_qkv,
    w_self_out,
    nbr_kv,
    nbr_count,
    nbr_source,
    span_order,
):
    tok_rows, model_width = hidden_in.shape
    features = w_cross_query.shape[1]
    heads_here = features // HD
    groups = lax.axis_size(("enc", "mp"))
    share_width = model_width // groups
    group_index = lax.axis_index(("enc", "mp"))
    column = lax.axis_index("ctx")
    attn_scale = 1.0 / math.sqrt(HD)
    normed = rms_rows(hidden_in, norm_gains[0])
    columns_part = normed
    cross_query = jnp.dot(
        columns_part,
        lax.all_gather(w_cross_query, "ctx", axis=0, tiled=True),
        preferred_element_type=jnp.float32,
    ).astype(jnp.bfloat16)
    arrived = lax.all_to_all(nbr_kv[0, 0], "enc", split_axis=0, concat_axis=0, tiled=True)
    sources, slot_count, nbr_rows, pair_width = arrived.shape
    flattened = arrived.reshape(sources * slot_count, nbr_rows, pair_width)
    spans_here, per_span = nbr_source.shape
    chosen = nbr_source.reshape(-1)
    matches = (chosen[:, None] == jnp.arange(sources, dtype=jnp.int32)[None, :]).astype(jnp.int32)
    earlier = jnp.cumsum(matches, axis=0) - matches
    places = chosen * slot_count + jnp.sum(earlier * matches, axis=1)
    picked = jnp.take(flattened, places, axis=0)
    picked = picked.reshape(spans_here, per_span, nbr_rows, heads_here, 2, HD)
    nbr_keys = picked[:, :, :, :, 0, :]
    nbr_values = picked[:, :, :, :, 1, :]
    queries = cross_query.reshape(spans_here, tok_rows // spans_here, heads_here, HD)
    scores = (
        jnp.einsum("cqhd,cjrhd->chqjr", queries, nbr_keys, preferred_element_type=jnp.float32)
        * attn_scale
    )
    alive_mask = jnp.arange(per_span, dtype=jnp.int32)[None, :] < nbr_count[:, None]
    scores = jnp.where(alive_mask[:, None, None, :, None], scores, far_below)
    row_top = jnp.max(scores, axis=(3, 4), keepdims=True)
    weights_f = jnp.exp(scores - row_top)
    row_total = jnp.sum(weights_f, axis=(3, 4))
    mixed_heads = (
        jnp.einsum(
            "chqjr,cjrhd->chqd",
            weights_f.astype(jnp.bfloat16),
            nbr_values,
            preferred_element_type=jnp.float32,
        )
        / row_total[..., None]
    )
    cross_att = mixed_heads.transpose(0, 2, 1, 3).reshape(tok_rows, features).astype(jnp.bfloat16)
    cross_term = jnp.dot(
        cross_att,
        lax.all_gather(w_cross_out, "ctx", axis=1, tiled=True),
        preferred_element_type=jnp.float32,
    )
    summed = lax.psum(cross_term.astype(jnp.bfloat16), ("enc", "mp")).astype(jnp.float32)
    mid_full = (hidden_in.astype(jnp.float32) + summed).astype(jnp.bfloat16)
    mid_normed = rms_rows(mid_full, norm_gains[1])
    mid_share = lax.dynamic_slice_in_dim(mid_full, group_index * share_width, share_width, 1)
    shard_piece = lax.all_gather(w_self_qkv, "ctx", axis=0, tiled=True)
    columns_part = mid_normed
    projected = jnp.dot(
        columns_part,
        shard_piece.reshape(shard_piece.shape[0], 3 * features),
        preferred_element_type=jnp.float32,
    )
    projected = projected.astype(jnp.bfloat16).reshape(tok_rows, 3, heads_here, HD)
    self_query = projected[:, 0]
    keys_values = projected[:, 1:]
    query_places = token_places(span_order, column * tok_rows, tok_rows)
    shard_piece = lax.all_gather(keys_values, "ctx", axis=0, tiled=True)
    old_top = jnp.full((heads_here, tok_rows), far_below, jnp.float32)
    key_places = token_places(span_order, jnp.int32(0), shard_piece.shape[0])
    block_scores = (
        jnp.einsum(
            "qhd,khd->hqk", self_query, shard_piece[:, 0], preferred_element_type=jnp.float32
        )
        * attn_scale
    )
    visible = key_places[None, None, :] <= query_places[None, :, None]
    block_scores = jnp.where(visible, block_scores, far_below)
    new_top = jnp.maximum(old_top, jnp.max(block_scores, axis=2))
    block_weights = jnp.where(visible, jnp.exp(block_scores - new_top[..., None]), 0.0)
    new_total = jnp.sum(block_weights, axis=2)
    running = jnp.einsum(
        "hqk,khd->hqd",
        block_weights.astype(jnp.bfloat16),
        shard_piece[:, 1],
        preferred_element_type=jnp.float32,
    )
    self_att = (
        (running / new_total[..., None])
        .transpose(1, 0, 2)
        .reshape(tok_rows, features)
        .astype(jnp.bfloat16)
    )
    self_term = jnp.dot(
        self_att,
        lax.all_gather(w_self_out, "ctx", axis=1, tiled=True),
        preferred_element_type=jnp.float32,
    )
    out_share = lax.psum_scatter(
        self_term.astype(jnp.bfloat16), ("enc", "mp"), scatter_dimension=1, tiled=True
    ).astype(jnp.float32)
    return (mid_share.astype(jnp.float32) + out_share).astype(jnp.bfloat16)


def dot(a, b):
    return jnp.dot(a, b, preferred_element_type=F32)


def dot_t(a, b):
    return lax.dot_general(a, b, (((1,), (1,)), ((), ())), preferred_element_type=F32)


def block_kernel(
    hid_in, gains, wq_in, wco_in, wqkv_in, wso, nbr, cnt, nsrc, order, out,
    hid, wq, wco, wqkv, hid_all, nbr_all, qsend, qpart, rs0, att_all, wso_all, term, corebuf, cs, rsbuf, mid_all,
    sssend, sspart, kvsend, kvpart, kvrelay, q2send, q2part, q2relay, qbuf, kv_all, midown, att2, fother, fmine, fcore, fsum, frs,
    send_sems, recv_sems, local_sems,
):
    c, e, m = lax.axis_index("ctx"), lax.axis_index("enc"), lax.axis_index("mp")
    n = hid_all.shape[0]
    tok, width = hid.shape
    shard = width // n
    feats = wq.shape[1]
    heads = feats // HD
    slots = nbr.shape[1]
    n_enc = nbr.shape[0]
    rows = tok // 8
    half = tok // 2
    cols = out.shape[1]
    attn_scale = 1.0 / math.sqrt(HD)

    core, y = lax.rem(e, 2), e // 2
    mate = {"enc": e + 1 - 2 * core}
    place = y * 2 + m

    def at_place(p):
        y2 = 1 - y if p & 2 else y
        m2 = 1 - m if p & 1 else m
        return y2, m2

    def peer(p):
        y2, m2 = at_place(p)
        return {"enc": y2 * 2 + core, "mp": m2}

    def ctx_of(k):
        return lax.rem(c + k, n)

    def src_of(k):
        return lax.rem(c - k + n, n)

    near = 3 - 2 * (c // 2)
    far = 4 - near
    is_inner = lax.rem((c + 1) // 2, 2)
    is_outer = 1 - is_inner
    inner, outer = is_inner == 1, is_outer == 1
    turns = [0, is_inner * near + is_outer * 2, far, is_inner * 2 + is_outer * near]

    issued = []
    count = [0]

    def alloc(amount):
        count[0] += amount
        return count[0] - amount

    def describe(src, dst, device, send, recv):
        return pltpu.make_async_remote_copy(
            src_ref=src, dst_ref=dst, send_sem=send_sems.at[send], recv_sem=recv_sems.at[recv],
            device_id=device, device_id_type=MESH,
        )

    def rcopy(src, dst, device):
        i = alloc(1)
        d = describe(src, dst, device, i, i)
        d.start()
        issued.append((None, d))
        return d

    def gather_start(src, buf, base, part=slice(None)):
        def one(k):
            return describe(src, buf.at[c, part], {"ctx": ctx_of(k)}, base + k - 1, base + k - 1)

        last = one(near)
        for d in (one(2), one(far)):
            d.start()
            issued.append((None, d))

        @pl.when(inner)
        def _():
            last.start()

        issued.append((inner, last))

    def gather_wait(buf, base, k, part=slice(None)):
        block = buf.at[c, part]
        describe(block, block, {"ctx": ctx_of(1)}, base, base + k - 1).wait_recv()

    def gather_relay(buf, base, part=slice(None)):
        block = buf.at[src_of(2), part]
        d = describe(block, block, {"ctx": (c - 1) * 3}, base + 3, base + 2 * is_inner * (c - 1))
        issued.append((inner, d))

        @pl.when(inner)
        def _():
            d.start()

    def scatter_send(turn, send, part, relay, base):
        k = turns[turn]
        s = src_of(k)
        at = base + turn - 1
        direct = describe(send.at[s], part.at[k - 1], {"ctx": s}, at, base + k - 1)
        via = describe(send.at[s], relay, {"ctx": 1 + c // 3}, at, base + 3)
        if turn == 2:
            @pl.when(outer)
            def _():
                via.start()

            @pl.when(inner)
            def _():
                direct.start()
        elif turn == 3:
            pl.when(outer)(direct.start)
        else:
            direct.start()
        issued.append((None, direct))

    def scatter_merge(send, part, relay, base):
        k = turns[3]
        s = src_of(k)
        direct = describe(send.at[s], part.at[k - 1], {"ctx": s}, base + 2, base + k - 1)
        via = describe(send.at[s], relay, {"ctx": 1 + c // 3}, base + 2, base + 3)

        @pl.when(inner)
        def _():
            via.wait_recv()
            send[s] = (send[s].astype(F32) + relay[...].astype(F32)).astype(BF16)
            direct.start()

    def scatter_wait(part, base):
        def one(k):
            block = part.at[0]
            describe(block, block, {"ctx": ctx_of(1)}, base, base + k - 1).wait_recv()

        one(2)
        one(far)

        @pl.when(inner)
        def _():
            one(near)

        @pl.when(outer)
        def _():
            part[near - 1] = jnp.zeros(part.shape[1:], BF16)

    barrier = pltpu.get_barrier_semaphore()
    friends = [{"ctx": ctx_of(k)} for k in range(1, n)]
    friends += [{"enc": lax.rem(e + k, n_enc)} for k in range(1, n_enc)]
    friends += [peer(1), peer(3)]
    for f in friends:
        pl.semaphore_signal(barrier, inc=1, device_id=f, device_id_type=MESH)
    pl.semaphore_wait(barrier, len(friends))

    my_rows = pl.ds(pl.multiple_of(core * half + place * rows, rows), rows)
    my_half = pl.ds(pl.multiple_of(core * half, half), half)
    mate_half = pl.ds(pl.multiple_of((1 - core) * half, half), half)
    my_shard = pl.ds(pl.multiple_of(c * shard, shard), shard)

    a1 = {}
    for k in range(1, n):
        t = ctx_of(k)
        there = pl.ds(pl.multiple_of(t * shard, shard), shard)
        a1[k] = rcopy(hid_in.at[my_rows, there], hid_all.at[c, my_rows, :], {"ctx": t})
    def fetch(i, src, dst):
        d = pltpu.make_async_copy(src, dst, local_sems.at[i])
        d.start()
        return d

    got_shard = fetch(0, hid_in.at[:, my_shard], hid_all.at[c])
    got_wq = fetch(1, wq_in, wq)
    got_hid = fetch(2, hid_in, hid)
    got_nbr = fetch(3, nbr.at[e], nbr_all.at[pl.ds(e * slots, slots)])
    got_wco = fetch(4, wco_in, wco)
    got_wqkv = fetch(5, wqkv_in, wqkv)
    got_wso = fetch(6, wso, wso_all.at[c])
    nb = []
    for k in range(1, n_enc):
        f = lax.rem(e + k, n_enc)
        nb.append(rcopy(nbr.at[f], nbr_all.at[pl.ds(e * slots, slots)], {"enc": f}))
    gain0 = gains[0:1, my_shard]
    gain1 = gains[1:2, my_shard]

    def project_query(s):
        x = (hid_all[s].astype(F32) * gain0).astype(BF16)
        qsend[s] = dot(x, wq[...]).astype(BF16)

    a2 = {}
    for k in range(1, n):
        s = src_of(k)
        a1[k].wait_recv()
        for p in (3, 1, 2):
            block = hid_all.at[s, my_rows, :]
            a2[k, p] = rcopy(block, block, peer(p))
    ws = (alloc(4), alloc(4))
    deep = feats // 2
    gather_start(wso.at[0:deep], wso_all, ws[0], pl.ds(0, deep))
    got_shard.wait()
    got_wq.wait()
    project_query(c)
    got_hid.wait()
    squares = jnp.zeros((tok, 1), F32)
    for j in range(n):
        x = hid[:, j * shard:(j + 1) * shard].astype(F32)
        squares = squares + jnp.sum(x * x, axis=1, keepdims=True)
    rs0[...] = jnp.broadcast_to(lax.rsqrt(squares / width + epsilon), rs0.shape)
    a3 = {}
    for k in range(1, n):
        s = src_of(k)
        for p in (1, 2, 3):
            a2[k, p].wait_recv()
        block = hid_all.at[s, my_half, :]
        a3[k] = rcopy(block, block, mate)
    qs = []
    for k in range(1, n):
        s = src_of(k)
        a3[k].wait_recv()
        project_query(s)
        qs.append(rcopy(qsend.at[s], qpart.at[k - 1], {"ctx": s}))
    got_nbr.wait()
    for d in nb:
        d.wait_recv()
    for d in qs:
        d.wait_recv()
    q = qsend[c].astype(F32)
    for k in range(n - 1):
        q = q + qpart[k].astype(F32)
    q = (q * rs0[:, 0:1]).astype(BF16)

    per_span, spans = nsrc.shape
    lane = lax.broadcasted_iota(jnp.int32, (SPAN, per_span * SPAN), 1)
    for i in range(spans):
        kv = []
        for j in range(per_span):
            chosen = nsrc[j, i]
            rank = 0
            for i2 in range(i):
                for j2 in range(per_span):
                    rank = rank + jnp.where(nsrc[j2, i2] == chosen, 1, 0)
            kv.append(nbr_all[chosen * slots + rank])
        alive = lane < cnt[i] * SPAN
        for u in range(heads):
            lo = 2 * u * HD
            keys = jnp.concatenate([b[:, lo:lo + HD] for b in kv], axis=0)
            values = jnp.concatenate([b[:, lo + HD:lo + 2 * HD] for b in kv], axis=0)
            qi = q[i * SPAN:(i + 1) * SPAN, u * HD:(u + 1) * HD]
            sc = jnp.where(alive, dot_t(qi, keys) * attn_scale, far_below)
            w = jnp.exp(sc - jnp.max(sc, axis=1, keepdims=True))
            mixed = dot(w.astype(BF16), values) / jnp.sum(w, axis=1, keepdims=True)
            att_all[c, i * SPAN:(i + 1) * SPAN, u * HD:(u + 1) * HD] = mixed.astype(BF16)

    at = alloc(3)
    for k in range(1, n):
        d = describe(att_all.at[c], att_all.at[c], {"ctx": ctx_of(k)}, at + k - 1, at + k - 1)
        d.start()
        issued.append((None, d))
    gather_start(wso.at[deep:], wso_all, ws[1], pl.ds(deep, deep))

    @pl.when(inner)
    def _():
        gather_wait(wso_all, ws[0], 2, pl.ds(0, deep))

    gather_relay(wso_all, ws[0], pl.ds(0, deep))
    got_wco.wait()
    got_wqkv.wait()

    c2, c3, c4, c5, ssp = {}, {}, {}, {}, []
    kvb, q2b = alloc(4), alloc(4)

    def project_out(j):
        s = src_of(turns[j])
        if j:
            gather_wait(att_all, at, turns[j])
        term[s] = dot(att_all[s], wco[...]).astype(BF16)
        c2[j] = rcopy(term.at[s, mate_half, :], corebuf.at[s], mate)

    def pair_sum(j):
        s = src_of(turns[j])
        c2[j].wait_recv()
        cs[s] = (term[s, my_half, :].astype(F32) + corebuf[s].astype(F32)).astype(BF16)
        for p in (3, 1, 2):
            y2, m2 = at_place(p)
            theirs = pl.ds(pl.multiple_of((y2 * 2 + m2) * rows, rows), rows)
            c3[j, p] = rcopy(cs.at[s, theirs, :], rsbuf.at[p - 1, s], peer(p))

    def plane_sum(j):
        s = src_of(turns[j])
        total = hid_all[s, my_rows, :].astype(F32)
        total = total + cs[s, pl.ds(pl.multiple_of(place * rows, rows), rows), :].astype(F32)
        for p in (1, 2, 3):
            c3[j, p].wait_recv()
            total = total + rsbuf[p - 1, s].astype(F32)
        mid_all[s, my_rows, :] = total.astype(BF16)
        block = mid_all.at[s, my_rows, :]
        for p in (3, 1, 2):
            c4[j, p] = rcopy(block, block, peer(p))

    def plane_share(j):
        s = src_of(turns[j])
        for p in (1, 2, 3):
            c4[j, p].wait_recv()
        block = mid_all.at[s, my_half, :]
        c5[j] = rcopy(block, block, mate)

    def project_kv(j):
        s = src_of(turns[j])
        c5[j].wait_recv()
        x = mid_all[s].astype(F32)
        squares = jnp.sum(x * x, axis=1, keepdims=True)
        sssend[s] = jnp.broadcast_to(squares, (tok, HD)).T[0:8]
        x = (x * gain1).astype(BF16)
        kvsend[s, :, 0:feats] = dot(x, wqkv[1]).astype(BF16)
        kvsend[s, :, feats:] = dot(x, wqkv[2]).astype(BF16)
        if j:
            scatter_send(j, kvsend, kvpart, kvrelay, kvb)
        if j == 3:
            scatter_merge(kvsend, kvpart, kvrelay, kvb)

    stages = (project_out, pair_sum, plane_sum, plane_share, project_kv)
    for step in range(n + len(stages) - 1):
        for i in reversed(range(len(stages))):
            if 0 <= step - i < n:
                stages[i](step - i)
    for k in range(1, n):
        s = src_of(k)
        ssp.append(rcopy(sssend.at[s], sspart.at[k - 1], {"ctx": s}))
    for j in (1, 2, 3, 0):
        s = src_of(turns[j])
        x = (mid_all[s].astype(F32) * gain1).astype(BF16)
        q2send[s] = dot(x, wqkv[0]).astype(BF16)
        if j:
            scatter_send(j, q2send, q2part, q2relay, q2b)
    my_cols = pl.ds(pl.multiple_of(m * cols, cols), cols)

    def whole(send, part):
        total = send[c].astype(F32)
        for k in range(n - 1):
            total = total + part[k].astype(F32)
        return (total * row_scale).astype(BF16)

    for d in ssp:
        d.wait_recv()
    squares = sssend[c]
    for k in range(n - 1):
        squares = squares + sspart[k]
    squares = jnp.broadcast_to(squares[0:1], (HD, tok)).T[:, 0:1]
    row_scale = lax.rsqrt(squares / width + epsilon)
    scatter_wait(kvpart, kvb)
    kv_all[c] = whole(kvsend, kvpart)
    kvg = alloc(4)
    gather_start(kv_all.at[c], kv_all, kvg)

    scatter_merge(q2send, q2part, q2relay, q2b)

    @pl.when(inner)
    def _():
        gather_wait(wso_all, ws[1], 2, pl.ds(deep, deep))

    gather_relay(wso_all, ws[1], pl.ds(deep, deep))

    resid = alloc(3)
    residual = []
    for k in range(1, n):
        t = ctx_of(k)
        residual.append(
            describe(mid_all.at[t, :, my_cols], midown, {"ctx": t}, resid + k - 1, resid)
        )

    @pl.when(c == e)
    def _():
        for d in residual:
            d.start()
        midown[...] = mid_all[c, :, my_cols]

    scatter_wait(q2part, q2b)
    qbuf[...] = whole(q2send, q2part)

    def places(s, shape, axis):
        index = lax.broadcasted_iota(jnp.int32, shape, axis)
        first = s * (tok // SPAN)
        found = jnp.zeros(shape, jnp.int32)
        for b in range(tok // SPAN):
            found = jnp.where(index // SPAN == b, order[first + b], found)
        return found * SPAN + lax.rem(index, SPAN)

    query_places = places(c, (tok, 1), 0)
    tops = [jnp.full((tok, 1), far_below, F32) for _ in range(heads)]
    sums = [jnp.zeros((tok, 1), F32) for _ in range(heads)]
    accs = [jnp.zeros((tok, HD), F32) for _ in range(heads)]
    arrivals = (0, is_inner * 2 + is_outer * near, is_inner * near + is_outer * 2, far)
    for i, k in enumerate(arrivals):
        s = src_of(k)
        if i:
            gather_wait(kv_all, kvg, k)
        if i == 1:
            gather_relay(kv_all, kvg)
        visible = places(s, (1, tok), 1) <= query_places
        for u in range(heads):
            keys = kv_all[s, :, u * HD:(u + 1) * HD]
            values = kv_all[s, :, feats + u * HD:feats + (u + 1) * HD]
            sc = dot_t(qbuf[:, u * HD:(u + 1) * HD], keys) * attn_scale
            sc = jnp.where(visible, sc, far_below)
            top = jnp.maximum(tops[u], jnp.max(sc, axis=1, keepdims=True))
            w = jnp.where(visible, jnp.exp(sc - top), 0.0)
            shrink = jnp.exp(tops[u] - top)
            sums[u] = sums[u] * shrink + jnp.sum(w, axis=1, keepdims=True)
            accs[u] = accs[u] * shrink + dot(w.astype(BF16), values)
            tops[u] = top
    for u in range(heads):
        att2[:, u * HD:(u + 1) * HD] = (accs[u] / sums[u]).astype(BF16)

    got_wso.wait()
    for i in range(2):
        part = pl.ds(i * deep, deep)
        gather_wait(wso_all, ws[i], near, part)
        gather_wait(wso_all, ws[i], far, part)

        @pl.when(outer)
        def _():
            gather_wait(wso_all, ws[i], 2, part)

    f1 = {}
    for p in (3, 1, 2, 0):
        y2, m2 = at_place(p)
        there = pl.ds(pl.multiple_of(m2 * cols, cols), cols)
        fother[p] = dot(att2[...], wso_all[y2 * 2 + 1 - core, :, there]).astype(BF16)
        f1[p] = rcopy(fother.at[p], fcore.at[p], mate)
        fmine[p] = dot(att2[...], wso_all[y2 * 2 + core, :, there]).astype(BF16)
    f2 = {}
    for p in (3, 1, 2):
        f1[p].wait_recv()
        fsum[p - 1] = (fmine[p].astype(F32) + fcore[p].astype(F32)).astype(BF16)
        f2[p] = rcopy(fsum.at[p - 1], frs.at[p - 1], peer(p))
    f1[0].wait_recv()

    @pl.when(c == e)
    def _():
        for d in residual:
            d.wait_send()

    @pl.when(c != e)
    def _():
        residual[0].wait_recv()

    total = midown[...].astype(F32) + fmine[0].astype(F32) + fcore[0].astype(F32)
    for p in (1, 2, 3):
        f2[p].wait_recv()
        total = total + frs[p - 1].astype(F32)
    out[...] = total.astype(BF16)
    for condition, d in issued:
        if condition is None:
            d.wait_send()
        else:
            pl.when(condition)(d.wait_send)


def scratch_shapes(n, n_enc, tok, width, feats, slots, nbr_rows, pair_width, cols):
    shard = width // n
    half, rows = tok // 2, tok // 8
    return [
        ((tok, width), BF16),
        ((shard, feats), BF16),
        ((feats, shard), BF16),
        ((3, shard, feats), BF16),
        ((n, tok, shard), BF16),
        ((n_enc * slots, nbr_rows, pair_width), BF16),
        ((n, tok, feats), BF16),
        ((n - 1, tok, feats), BF16),
        ((tok, HD), F32),
        ((n, tok, feats), BF16),
        ((n, feats, shard), BF16),
        ((n, tok, shard), BF16),
        ((n, half, shard), BF16),
        ((n, half, shard), BF16),
        ((3, n, rows, shard), BF16),
        ((n, tok, shard), BF16),
        ((n, 8, tok), F32),
        ((n - 1, 8, tok), F32),
        ((n, tok, 2 * feats), BF16),
        ((n - 1, tok, 2 * feats), BF16),
        ((tok, 2 * feats), BF16),
        ((n, tok, feats), BF16),
        ((n - 1, tok, feats), BF16),
        ((tok, feats), BF16),
        ((tok, feats), BF16),
        ((n, tok, 2 * feats), BF16),
        ((tok, cols), BF16),
        ((tok, feats), BF16),
        ((4, tok, cols), BF16),
        ((4, tok, cols), BF16),
        ((4, tok, cols), BF16),
        ((3, tok, cols), BF16),
        ((3, tok, cols), BF16),
    ]


def per_device_any(sizes, *args):
    n, n_enc, n_mp = sizes
    hidden_in, norm_gains, w_cross_query, w_cross_out, w_self_qkv, w_self_out, nbr_kv = args[:7]
    tok, width = hidden_in.shape
    feats = w_cross_query.shape[1]
    cols = width // (n_enc * n_mp)
    slots, nbr_rows, pair_width = nbr_kv.shape[3:]
    held = scratch_shapes(n, n_enc, tok, width, feats, slots, nbr_rows, pair_width, cols)
    need = sum(math.prod(shape) * jnp.dtype(kind).itemsize for shape, kind in held)
    if need > VMEM_GRANT // 2 or sizes != (4, 4, 2) or width != n * 2 * cols:
        return per_device(*args)
    copies = 128
    vmem = pl.BlockSpec(memory_space=pltpu.VMEM)
    smem = pl.BlockSpec(memory_space=pltpu.SMEM)
    hbm = pl.BlockSpec(memory_space=pl.ANY)
    return pl.pallas_call(
        block_kernel,
        out_shape=jax.ShapeDtypeStruct((tok, cols), BF16),
        in_specs=[hbm, vmem, hbm, hbm, hbm, hbm, hbm] + [smem] * 3,
        out_specs=vmem,
        scratch_shapes=[pltpu.VMEM(shape, kind) for shape, kind in held]
        + [pltpu.SemaphoreType.DMA((copies,)), pltpu.SemaphoreType.DMA((copies,))]
        + [pltpu.SemaphoreType.DMA((8,))],
        compiler_params=pltpu.CompilerParams(
            collective_id=0, has_side_effects=True, vmem_limit_bytes=VMEM_GRANT
        ),
    )(
        hidden_in, norm_gains, w_cross_query, w_cross_out,
        jnp.transpose(w_self_qkv, (1, 0, 2)), w_self_out,
        nbr_kv[0, 0], args[7], args[8].T, args[9],
    )


def solution(mesh):
    in_specs = (
        P("ctx", None),
        P(),
        P("ctx", ("enc", "mp")),
        P(("enc", "mp"), "ctx"),
        P("ctx", None, ("enc", "mp")),
        P(("enc", "mp"), "ctx"),
        P("ctx", "enc", None, None, None, "mp"),
        P("ctx"),
        P("ctx", None),
        P(),
    )
    out_specs = P("ctx", ("enc", "mp"))
    sizes = (mesh.shape["ctx"], mesh.shape["enc"], mesh.shape["mp"])
    return jax.shard_map(
        functools.partial(per_device_any, sizes), mesh=mesh, in_specs=in_specs, out_specs=out_specs, check_vma=False
    )
```

profile of v0, /device:TPU:0, one launch (start us, length us, event | category | flops | bytes accessed | tf_op | source)
XLA Modules:
  0.0 152.0 jit_solution(2872294591557632528)
XLA Ops:
  0.0 150.3 %shard_map.100 = bf16[256,512]{1,0:T(8,128)(2,1)} custom-call(bf16[256,4096]{1,0:T(8,128)(2,1)} %hid_in.1, f32[2,4096]{1,0:T(2,128)} %gains.1, bf16[1024,256]{1,0:T(8,128)(2,1)} %wq_in.1, bf16[256,1024]{1,0:T(8,128)(2,1)} %wco_in.1, bf16[3,1024,256]{2,1,0:T(8,128)(2,1)} %bitcast.3, bf16[256,1024]{1,0:T(8,128)(2,1)} %wso.1, bf16[4,3,64,512]{3,2,1,0:T(8,128)(2,1)} %bitcast.4, ...), custom_call_target="tpu_custom_call" | custom-call | tf_op jit(solution)/shard_map/pallas_call | solution.py:668
  150.3 1.7 %copy.12 = bf16[256,512]{1,0:T(8,128)(2,1)} copy(bf16[256,512]{1,0:T(8,128)(2,1)} %shard_map.100) | data formatting | bytes 524288
where the time goes:
time: 152 us
  Pallas kernels  150 us (99%)
  local copies, waits for them, and re-layouts  1.67 us (1%)
    pallas_call x1, Pallas kernels, per_device_any(): pl.pallas_call(block_kernel, out_shape=jax.ShapeDtypeStruct((tok, cols),...  150 us

commit v1 on v0

--- a/solution.py
+++ b/solution.py
@@ -162,7 +162,7 @@
 def block_kernel(
     hid_in, gains, wq_in, wco_in, wqkv_in, wso, nbr, cnt, nsrc, order, out,
     hid, wq, wco, wqkv, hid_all, nbr_all, qsend, qpart, rs0, att_all, wso_all, term, corebuf, cs, rsbuf, mid_all,
-    sssend, sspart, kvsend, kvpart, kvrelay, q2send, q2part, q2relay, qbuf, kv_all, midown, att2, fother, fmine, fcore, fsum, frs,
+    sssend, sspart, kvsend, kvpart, kvrelay, q2send, q2part, q2relay, qbuf, kv_all, midown, att2, fother, fcore, fsum, frs,
     send_sems, recv_sems, local_sems,
 ):
     c, e, m = lax.axis_index("ctx"), lax.axis_index("enc"), lax.axis_index("mp")
@@ -313,11 +313,16 @@
     mate_half = pl.ds(pl.multiple_of((1 - core) * half, half), half)
     my_shard = pl.ds(pl.multiple_of(c * shard, shard), shard)
 
-    a1 = {}
+    a1 = alloc(3)
     for k in range(1, n):
         t = ctx_of(k)
         there = pl.ds(pl.multiple_of(t * shard, shard), shard)
-        a1[k] = rcopy(hid_in.at[my_rows, there], hid_all.at[c, my_rows, :], {"ctx": t})
+        d = describe(
+            hid_in.at[my_rows, there], hid_all.at[c, my_rows, :], {"ctx": t}, a1 + k - 1, a1 + k - 1
+        )
+        d.start()
+        issued.append((None, d))
+    nearest = {1: near, 2: is_inner * far + is_outer * 2, 3: is_inner * 2 + is_outer * far}
     def fetch(i, src, dst):
         d = pltpu.make_async_copy(src, dst, local_sems.at[i])
         d.start()
@@ -343,8 +348,8 @@
 
     a2 = {}
     for k in range(1, n):
-        s = src_of(k)
-        a1[k].wait_recv()
+        s = src_of(nearest[k])
+        gather_wait(hid_all, a1, nearest[k], my_rows)
         for p in (3, 1, 2):
             block = hid_all.at[s, my_rows, :]
             a2[k, p] = rcopy(block, block, peer(p))
@@ -362,22 +367,25 @@
     rs0[...] = jnp.broadcast_to(lax.rsqrt(squares / width + epsilon), rs0.shape)
     a3 = {}
     for k in range(1, n):
-        s = src_of(k)
+        s = src_of(nearest[k])
         for p in (1, 2, 3):
             a2[k, p].wait_recv()
         block = hid_all.at[s, my_half, :]
         a3[k] = rcopy(block, block, mate)
-    qs = []
-    for k in range(1, n):
+    qs = alloc(3)
+    for j in range(1, n):
+        k = nearest[j]
         s = src_of(k)
-        a3[k].wait_recv()
+        a3[j].wait_recv()
         project_query(s)
-        qs.append(rcopy(qsend.at[s], qpart.at[k - 1], {"ctx": s}))
+        d = describe(qsend.at[s], qpart.at[k - 1], {"ctx": s}, qs + j - 1, qs + k - 1)
+        d.start()
+        issued.append((None, d))
     got_nbr.wait()
     for d in nb:
         d.wait_recv()
-    for d in qs:
-        d.wait_recv()
+    for k in range(1, n):
+        gather_wait(qsend, qs, k)
     q = qsend[c].astype(F32)
     for k in range(n - 1):
         q = q + qpart[k].astype(F32)
@@ -385,6 +393,7 @@
 
     per_span, spans = nsrc.shape
     lane = lax.broadcasted_iota(jnp.int32, (SPAN, per_span * SPAN), 1)
+    blocks = []
     for i in range(spans):
         kv = []
         for j in range(per_span):
@@ -394,16 +403,24 @@
                 for j2 in range(per_span):
                     rank = rank + jnp.where(nsrc[j2, i2] == chosen, 1, 0)
             kv.append(nbr_all[chosen * slots + rank])
-        alive = lane < cnt[i] * SPAN
-        for u in range(heads):
-            lo = 2 * u * HD
-            keys = jnp.concatenate([b[:, lo:lo + HD] for b in kv], axis=0)
-            values = jnp.concatenate([b[:, lo + HD:lo + 2 * HD] for b in kv], axis=0)
+        blocks.append(jnp.concatenate(kv, axis=0))
+    for u in range(heads):
+        lo = 2 * u * HD
+        sc = []
+        for i in range(spans):
             qi = q[i * SPAN:(i + 1) * SPAN, u * HD:(u + 1) * HD]
-            sc = jnp.where(alive, dot_t(qi, keys) * attn_scale, far_below)
-            w = jnp.exp(sc - jnp.max(sc, axis=1, keepdims=True))
-            mixed = dot(w.astype(BF16), values) / jnp.sum(w, axis=1, keepdims=True)
-            att_all[c, i * SPAN:(i + 1) * SPAN, u * HD:(u + 1) * HD] = mixed.astype(BF16)
+            si = dot_t(qi, blocks[i][:, lo:lo + HD]) * attn_scale
+            sc.append(jnp.where(lane < cnt[i] * SPAN, si, far_below))
+        sc = jnp.concatenate(sc, axis=0)
+        w = jnp.exp(sc - jnp.max(sc, axis=1, keepdims=True))
+        total = jnp.sum(w, axis=1, keepdims=True)
+        w = w.astype(BF16)
+        mixed = [
+            dot(w[i * SPAN:(i + 1) * SPAN], blocks[i][:, lo + HD:lo + 2 * HD])
+            for i in range(spans)
+        ]
+        mixed = jnp.concatenate(mixed, axis=0) / total
+        att_all[c, :, u * HD:(u + 1) * HD] = mixed.astype(BF16)
 
     at = alloc(3)
     for k in range(1, n):
@@ -575,18 +592,26 @@
         def _():
             gather_wait(wso_all, ws[i], 2, part)
 
-    f1 = {}
-    for p in (3, 1, 2, 0):
+    f1, f2 = {}, {}
+
+    def out_term(p, which):
         y2, m2 = at_place(p)
         there = pl.ds(pl.multiple_of(m2 * cols, cols), cols)
-        fother[p] = dot(att2[...], wso_all[y2 * 2 + 1 - core, :, there]).astype(BF16)
+        return dot(att2[...], wso_all[y2 * 2 + which, :, there])
+
+    def to_mate(p):
+        fother[p] = out_term(p, 1 - core).astype(BF16)
         f1[p] = rcopy(fother.at[p], fcore.at[p], mate)
-        fmine[p] = dot(att2[...], wso_all[y2 * 2 + core, :, there]).astype(BF16)
-    f2 = {}
+
     for p in (3, 1, 2):
+        to_mate(p)
+    for p in (3, 1, 2):
+        mine = out_term(p, core)
         f1[p].wait_recv()
-        fsum[p - 1] = (fmine[p].astype(F32) + fcore[p].astype(F32)).astype(BF16)
+        fsum[p - 1] = (mine + fcore[p].astype(F32)).astype(BF16)
         f2[p] = rcopy(fsum.at[p - 1], frs.at[p - 1], peer(p))
+    to_mate(0)
+    mine = out_term(0, core)
     f1[0].wait_recv()
 
     @pl.when(c == e)
@@ -598,7 +623,7 @@
     def _():
         residual[0].wait_recv()
 
-    total = midown[...].astype(F32) + fmine[0].astype(F32) + fcore[0].astype(F32)
+    total = midown[...].astype(F32) + mine + fcore[0].astype(F32)
     for p in (1, 2, 3):
         f2[p].wait_recv()
         total = total + frs[p - 1].astype(F32)
@@ -644,7 +669,6 @@
         ((tok, feats), BF16),
         ((4, tok, cols), BF16),
         ((4, tok, cols), BF16),
-        ((4, tok, cols), BF16),
         ((3, tok, cols), BF16),
         ((3, tok, cols), BF16),
     ]

time: 152 us -> 152 us (level)
  no operation moved by 1% of the time
where the time goes in v1:
time: 152 us; the launch traced here: 151 us
  Pallas kernels  150 us (99%)
  local copies, waits for them, and re-layouts  1.67 us (1%)
    pallas_call x1, Pallas kernels, per_device_any(): pl.pallas_call(block_kernel, out_shape=jax.ShapeDtypeStruct((tok, cols),...  150 us

profile of v1, /device:TPU:0, one launch (start us, length us, event | category | flops | bytes accessed | tf_op | source)
XLA Modules:
  0.0 151.3 jit_solution(4299877795069315941)
XLA Ops:
  0.0 149.6 %shard_map.100 = bf16[256,512]{1,0:T(8,128)(2,1)} custom-call(bf16[256,4096]{1,0:T(8,128)(2,1)} %hid_in.1, f32[2,4096]{1,0:T(2,128)} %gains.1, bf16[1024,256]{1,0:T(8,128)(2,1)} %wq_in.1, bf16[256,1024]{1,0:T(8,128)(2,1)} %wco_in.1, bf16[3,1024,256]{2,1,0:T(8,128)(2,1)} %bitcast.3, bf16[256,1024]{1,0:T(8,128)(2,1)} %wso.1, bf16[4,3,64,512]{3,2,1,0:T(8,128)(2,1)} %bitcast.4, ...), custom_call_target="tpu_custom_call" | custom-call | tf_op jit(solution)/shard_map/pallas_call | solution.py:692
  149.6 1.7 %copy.12 = bf16[256,512]{1,0:T(8,128)(2,1)} copy(bf16[256,512]{1,0:T(8,128)(2,1)} %shard_map.100) | data formatting | bytes 524288

commit v2 on v1

--- a/solution.py
+++ b/solution.py
@@ -503,6 +503,12 @@
         q2send[s] = dot(x, wqkv[0]).astype(BF16)
         if j:
             scatter_send(j, q2send, q2part, q2relay, q2b)
+    @pl.when(inner)
+    def _():
+        gather_wait(wso_all, ws[1], 2, pl.ds(deep, deep))
+
+    gather_relay(wso_all, ws[1], pl.ds(deep, deep))
+
     my_cols = pl.ds(pl.multiple_of(m * cols, cols), cols)
 
     def whole(send, part):
@@ -525,28 +531,25 @@
 
     scatter_merge(q2send, q2part, q2relay, q2b)
 
-    @pl.when(inner)
-    def _():
-        gather_wait(wso_all, ws[1], 2, pl.ds(deep, deep))
-
-    gather_relay(wso_all, ws[1], pl.ds(deep, deep))
+
+    scatter_wait(q2part, q2b)
+    qbuf[...] = whole(q2send, q2part)
 
     resid = alloc(3)
     residual = []
-    for k in range(1, n):
-        t = ctx_of(k)
-        residual.append(
-            describe(mid_all.at[t, :, my_cols], midown, {"ctx": t}, resid + k - 1, resid)
-        )
-
-    @pl.when(c == e)
-    def _():
-        for d in residual:
-            d.start()
-        midown[...] = mid_all[c, :, my_cols]
-
-    scatter_wait(q2part, q2b)
-    qbuf[...] = whole(q2send, q2part)
+
+    def send_residual():
+        for k in range(1, n):
+            t = ctx_of(k)
+            residual.append(
+                describe(mid_all.at[t, :, my_cols], midown, {"ctx": t}, resid + k - 1, resid)
+            )
+
+        @pl.when(c == e)
+        def _():
+            for d in residual:
+                d.start()
+            midown[...] = mid_all[c, :, my_cols]
 
     def places(s, shape, axis):
         index = lax.broadcasted_iota(jnp.int32, shape, axis)
@@ -567,6 +570,8 @@
             gather_wait(kv_all, kvg, k)
         if i == 1:
             gather_relay(kv_all, kvg)
+        if i == n - 1:
+            send_residual()
         visible = places(s, (1, tok), 1) <= query_places
         for u in range(heads):
             keys = kv_all[s, :, u * HD:(u + 1) * HD]

time: 152 us -> 146 us (0.961)
  Pallas kernels: 150 us -> 144 us
    pallas_call x1, Pallas kernels: 150 us -> 144 us  [per_device_any(): pl.pallas_call(block_kernel, out_shape=jax.ShapeDtypeStruct((tok, cols),...]
where the time goes in v2:
time: 146 us
  Pallas kernels  144 us (99%)
  local copies, waits for them, and re-layouts  1.67 us (1%)
    pallas_call x1, Pallas kernels, per_device_any(): pl.pallas_call(block_kernel, out_shape=jax.ShapeDtypeStruct((tok, cols),...  144 us

profile of v2, /device:TPU:0, one launch (start us, length us, event | category | flops | bytes accessed | tf_op | source)
XLA Modules:
  0.0 145.7 jit_solution(4222910984914861556)
XLA Ops:
  0.0 144.0 %shard_map.100 = bf16[256,512]{1,0:T(8,128)(2,1)} custom-call(bf16[256,4096]{1,0:T(8,128)(2,1)} %hid_in.1, f32[2,4096]{1,0:T(2,128)} %gains.1, bf16[1024,256]{1,0:T(8,128)(2,1)} %wq_in.1, bf16[256,1024]{1,0:T(8,128)(2,1)} %wco_in.1, bf16[3,1024,256]{2,1,0:T(8,128)(2,1)} %bitcast.3, bf16[256,1024]{1,0:T(8,128)(2,1)} %wso.1, bf16[4,3,64,512]{3,2,1,0:T(8,128)(2,1)} %bitcast.4, ...), custom_call_target="tpu_custom_call" | custom-call | tf_op jit(solution)/shard_map/pallas_call | solution.py:697
  144.0 1.7 %copy.12 = bf16[256,512]{1,0:T(8,128)(2,1)} copy(bf16[256,512]{1,0:T(8,128)(2,1)} %shard_map.100) | data formatting | bytes 524288

commit v3 on v2

--- a/solution.py
+++ b/solution.py
@@ -161,7 +161,7 @@
 
 def block_kernel(
     hid_in, gains, wq_in, wco_in, wqkv_in, wso, nbr, cnt, nsrc, order, out,
-    hid, wq, wco, wqkv, hid_all, nbr_all, qsend, qpart, rs0, att_all, wso_all, term, corebuf, cs, rsbuf, mid_all,
+    hid, wq, wco, wqkv, hid_all, nbr_all, qsend, qpart, qrelay, rs0, att_all, wso_all, term, corebuf, cs, rsbuf, mid_all,
     sssend, sspart, kvsend, kvpart, kvrelay, q2send, q2part, q2relay, qbuf, kv_all, midown, att2, fother, fcore, fsum, frs,
     send_sems, recv_sems, local_sems,
 ):
@@ -322,7 +322,6 @@
         )
         d.start()
         issued.append((None, d))
-    nearest = {1: near, 2: is_inner * far + is_outer * 2, 3: is_inner * 2 + is_outer * far}
     def fetch(i, src, dst):
         d = pltpu.make_async_copy(src, dst, local_sems.at[i])
         d.start()
@@ -348,8 +347,8 @@
 
     a2 = {}
     for k in range(1, n):
-        s = src_of(nearest[k])
-        gather_wait(hid_all, a1, nearest[k], my_rows)
+        s = src_of(turns[k])
+        gather_wait(hid_all, a1, turns[k], my_rows)
         for p in (3, 1, 2):
             block = hid_all.at[s, my_rows, :]
             a2[k, p] = rcopy(block, block, peer(p))
@@ -367,25 +366,21 @@
     rs0[...] = jnp.broadcast_to(lax.rsqrt(squares / width + epsilon), rs0.shape)
     a3 = {}
     for k in range(1, n):
-        s = src_of(nearest[k])
+        s = src_of(turns[k])
         for p in (1, 2, 3):
             a2[k, p].wait_recv()
         block = hid_all.at[s, my_half, :]
         a3[k] = rcopy(block, block, mate)
-    qs = alloc(3)
+    qs = alloc(4)
     for j in range(1, n):
-        k = nearest[j]
-        s = src_of(k)
         a3[j].wait_recv()
-        project_query(s)
-        d = describe(qsend.at[s], qpart.at[k - 1], {"ctx": s}, qs + j - 1, qs + k - 1)
-        d.start()
-        issued.append((None, d))
+        project_query(src_of(turns[j]))
+        scatter_send(j, qsend, qpart, qrelay, qs)
+    scatter_merge(qsend, qpart, qrelay, qs)
     got_nbr.wait()
     for d in nb:
         d.wait_recv()
-    for k in range(1, n):
-        gather_wait(qsend, qs, k)
+    scatter_wait(qpart, qs)
     q = qsend[c].astype(F32)
     for k in range(n - 1):
         q = q + qpart[k].astype(F32)
@@ -422,11 +417,8 @@
         mixed = jnp.concatenate(mixed, axis=0) / total
         att_all[c, :, u * HD:(u + 1) * HD] = mixed.astype(BF16)
 
-    at = alloc(3)
-    for k in range(1, n):
-        d = describe(att_all.at[c], att_all.at[c], {"ctx": ctx_of(k)}, at + k - 1, at + k - 1)
-        d.start()
-        issued.append((None, d))
+    at = alloc(4)
+    gather_start(att_all.at[c], att_all, at)
     gather_start(wso.at[deep:], wso_all, ws[1], pl.ds(deep, deep))
 
     @pl.when(inner)
@@ -442,7 +434,9 @@
 
     def project_out(j):
         s = src_of(turns[j])
-        if j:
+        if j == n - 1:
+            pl.when(outer)(lambda: gather_wait(att_all, at, near))
+        elif j:
             gather_wait(att_all, at, turns[j])
         term[s] = dot(att_all[s], wco[...]).astype(BF16)
         c2[j] = rcopy(term.at[s, mate_half, :], corebuf.at[s], mate)
@@ -491,6 +485,9 @@
 
     stages = (project_out, pair_sum, plane_sum, plane_share, project_kv)
     for step in range(n + len(stages) - 1):
+        if step == 2:
+            pl.when(inner)(lambda: gather_wait(att_all, at, 2))
+            gather_relay(att_all, at)
         for i in reversed(range(len(stages))):
             if 0 <= step - i < n:
                 stages[i](step - i)
@@ -652,6 +649,7 @@
         ((n_enc * slots, nbr_rows, pair_width), BF16),
         ((n, tok, feats), BF16),
         ((n - 1, tok, feats), BF16),
+        ((tok, feats), BF16),
         ((tok, HD), F32),
         ((n, tok, feats), BF16),
         ((n, feats, shard), BF16),

time: 146 us -> 148 us (1.014)
  the two profiles are of different devices: /device:TPU:0 before, /device:TPU:5 now
where the time goes in v3:
time: 148 us; the launch traced here: 147 us
  Pallas kernels  146 us (99%)
  local copies, waits for them, and re-layouts  1.67 us (1%)
    pallas_call x1, Pallas kernels, per_device_any(): pl.pallas_call(block_kernel, out_shape=jax.ShapeDtypeStruct((tok, cols),...  146 us

profile of v3, /device:TPU:5, one launch (start us, length us, event | category | flops | bytes accessed | tf_op | source)
XLA Modules:
  0.0 147.4 jit_solution(15107868239401814242)
XLA Ops:
  0.0 145.7 %shard_map.100 = bf16[256,512]{1,0:T(8,128)(2,1)} custom-call(bf16[256,4096]{1,0:T(8,128)(2,1)} %hid_in.1, f32[2,4096]{1,0:T(2,128)} %gains.1, bf16[1024,256]{1,0:T(8,128)(2,1)} %wq_in.1, bf16[256,1024]{1,0:T(8,128)(2,1)} %wco_in.1, bf16[3,1024,256]{2,1,0:T(8,128)(2,1)} %bitcast.3, bf16[256,1024]{1,0:T(8,128)(2,1)} %wso.1, bf16[4,3,64,512]{3,2,1,0:T(8,128)(2,1)} %bitcast.4, ...), custom_call_target="tpu_custom_call" | custom-call | tf_op jit(solution)/shard_map/pallas_call | solution.py:695
  145.7 1.7 %copy.12 = bf16[256,512]{1,0:T(8,128)(2,1)} copy(bf16[256,512]{1,0:T(8,128)(2,1)} %shard_map.100) | data formatting | bytes 524288
